TPU v7x, 512 devices: a whole 4x8x8 slice. The times are simulated.
512 devices in a mesh: row: 32 (over y, x), col: 16 (over z, core).
Axes of the slice: x: 4, y: 8, z: 8, core: 2. Of those that a mesh axis runs over, the one named last changes fastest.
Arguments:
- momentum: float32 [8192, 26624], P('row', 'col')
- weight: bfloat16 [8192, 26624], P('row', 'col'), may hold values from -6 to 6
- init_seed: int32 [1], replicated, may hold values from 0 to 999999
- step_rate: float32 [1], replicated, may hold values from 0.1 to 1
Outputs:
- momentum_next: float32 [8192, 26624], P('row', 'col')
- weight_next: bfloat16 [8192, 26624], P('row', 'col')
- next_factor: float32 [512, 26624], P('row', 'col')
All inputs are finite; a program needn't handle non-finite values.
Results may differ from a plain program's by a relative error of at most 0.001.
Values sent between devices are 32-bit elements; how exact they have to be, the bound alone decides.
A program may use at most 64 MiB of HBM per device.

v0:
```python
import jax
import jax.numpy as jnp
from jax import lax
from jax.sharding import PartitionSpec as P

ROWS = 8192
COLS = 26624
RANK = 512


MOMENTUM_DECAY = 0.95
EPSILON = 1e-06
HIGHEST = lax.Precision.HIGHEST


def hashed(flat_index, seed_value):
    mixed = flat_index * 747796405 + seed_value * 277803737 + 1013904223
    mixed = jnp.bitwise_xor(mixed, jnp.right_shift(mixed, 15))
    mixed = mixed * 1664525
    mixed = jnp.bitwise_xor(mixed, jnp.right_shift(mixed, 13))
    return (mixed % 65536).astype(jnp.float32) / 32768.0 - 1.0


def seed_block(seed_value, first_col, col_count, rank_count):
    columns = lax.iota(jnp.int32, col_count) + first_col
    flat_index = columns[:, None] * rank_count + lax.iota(jnp.int32, rank_count)[None, :]
    return hashed(flat_index, seed_value)


def inner_rows(left, right_side):
    return lax.dot_general(left, right_side, (((0,), (0,)), ((), ())), precision=HIGHEST)


def orthonormal(projected, gram_matrix):
    factor_low = jnp.linalg.cholesky(gram_matrix)
    return jax.scipy.linalg.solve_triangular(factor_low, projected.T, lower=True).T


def per_device(momentum, weight, init_seed, step_rate):
    rows_local, cols_local = momentum.shape
    rank_count = RANK
    first_col = lax.axis_index("col") * cols_local
    start_factor = seed_block(init_seed[0], first_col, cols_local, rank_count)
    partial_proj = jnp.dot(momentum, start_factor, precision=HIGHEST)
    projected = lax.psum(partial_proj, "col")
    gram_matrix = lax.psum(inner_rows(projected, projected), "row")
    ortho_basis = orthonormal(projected, gram_matrix)
    rank_local = rank_count // lax.axis_size("row")
    right_share = lax.psum_scatter(
        inner_rows(momentum, ortho_basis), "row", scatter_dimension=0, tiled=True
    )
    square_sums = lax.psum(jnp.sum(right_share * right_share, axis=0), ("row", "col"))
    scale = lax.rsqrt(square_sums / COLS + EPSILON)
    right_factor = lax.all_gather(right_share, "row", axis=0, tiled=True)
    local_factor = right_factor * scale[None, :]
    rank_begin = lax.axis_index("row") * rank_local
    next_factor = lax.dynamic_slice_in_dim(local_factor, rank_begin, rank_local, 1).T
    feedback = lax.dot_general(
        ortho_basis, right_factor, (((1,), (1,)), ((), ())), precision=HIGHEST
    )
    update = lax.dot_general(ortho_basis, local_factor, (((1,), (1,)), ((), ())), precision=HIGHEST)
    momentum_next = momentum - (1.0 - MOMENTUM_DECAY) * feedback
    update = update * (ROWS / RANK) ** 0.5
    weight_next = (weight.astype(jnp.float32) - step_rate[0] * update).astype(jnp.bfloat16)
    return (momentum_next, weight_next, next_factor)


def solution(mesh):
    placed = (P("row", "col"), P("row", "col"), P(), P())
    return jax.shard_map(
        per_device,
        mesh=mesh,
        in_specs=placed,
        out_specs=(P("row", "col"), P("row", "col"), P("row", "col")),
        check_vma=False,
    )
```

profile of v0, /device:TPU:1, one launch (start us, length us, event | category | flops | bytes accessed | tf_op | source)
XLA Modules:
  0.0 760.9 jit_solution(4804314355737373489)
XLA Ops:
  7.2 0.0 all-reduce.6.cloned.1.call-start
  7.9 10.1 %fusion.25 = f32[256,512]{0,1:T(8,128)} fusion(f32[256,1664]{1,0:T(8,128)} %param.4, s32[]{:T(128)} %bitcast, s32[1664]{0:T(1024)S(1)} %add_multiply_fusion), kind=kOutput, calls=%fused_computation.35 | convolution fusion | flops 2636840960 | bytes 2234884 | tf_op jit(solution)/shard_map/dot_general | solution.py:44
  18.0 0.0 all-reduce.8.cloned.1.call-start
  18.1 121.4 %all-reduce.6.cloned.1.call-done = f32[256,512]{0,1:T(8,128)} async-done(((f32[256,512]{0,1:T(8,128)}), f32[256,512]{0,1:T(8,128)}) %all-reduce.6.cloned.1.call-update) | async-done | bytes 524304 | tf_op jit(solution)/shard_map/psum | solution.py:45
  139.5 3.2 fusion.72
  142.8 0.5 all-reduce.10.cloned.1.call-start
  143.3 156.2 %all-reduce.8.cloned.1.call-done = f32[512,512]{0,1:T(8,128)} async-done(((f32[512,512]{0,1:T(8,128)}), f32[512,512]{0,1:T(8,128)}) %all-reduce.8.cloned.1.call-update) | async-done | bytes 1048592 | tf_op jit(solution)/shard_map/psum | solution.py:46
  299.5 1.6 copy.14
  301.1 1.4 fusion.28
  302.5 1.0 copy-done.5
  303.5 11.7 %cholesky.104 = f32[128,128]{1,0:T(8,128)S(1)} custom-call(f32[128,128]{1,0:T(8,128)S(1)} %cholesky.266), custom_call_target="Cholesky" | custom-call | tf_op jit(solution)/shard_map/jit(cholesky)/cholesky | solution.py:35
  315.3 0.1 cholesky.224
  315.4 9.8 %custom-call.31 = f32[1,128,128]{1,2,0:T(8,128)S(1)} custom-call(f32[1,128,128]{2,1,0:T(8,128)S(1)} %get-tuple-element.38), custom_call_target="InvertDiagBlocksLowerTriangular" | custom-call | tf_op jit(solution)/shard_map/jit(cholesky)/cholesky | solution.py:35
  325.2 1.2 constant_dynamic-update-slice_fusion.3
  326.5 1.3 convolution_subtract_fusion
  327.7 11.7 %cholesky.217 = f32[128,128]{1,0:T(8,128)S(1)} custom-call(f32[128,128]{1,0:T(8,128)S(1)} %cholesky.270), custom_call_target="Cholesky" | custom-call | tf_op jit(solution)/shard_map/jit(cholesky)/cholesky | solution.py:35
  339.5 10.0 %custom-call.32 = f32[1,128,128]{1,2,0:T(8,128)S(1)} custom-call(f32[1,128,128]{2,1,0:T(8,128)S(1)} %get-tuple-element.35), custom_call_target="InvertDiagBlocksLowerTriangular" | custom-call | tf_op jit(solution)/shard_map/jit(cholesky)/cholesky | solution.py:35
  349.5 0.3 convolution_dynamic-update-slice_fusion
  349.7 1.3 convolution_subtract_fusion.3
  351.0 11.7 %cholesky.238 = f32[128,128]{1,0:T(8,128)S(1)} custom-call(f32[128,128]{1,0:T(8,128)S(1)} %cholesky.275), custom_call_target="Cholesky" | custom-call | tf_op jit(solution)/shard_map/jit(cholesky)/cholesky | solution.py:35
  362.8 9.8 %custom-call.33 = f32[1,128,128]{1,2,0:T(8,128)S(1)} custom-call(f32[1,128,128]{2,1,0:T(8,128)S(1)} %get-tuple-element.32), custom_call_target="InvertDiagBlocksLowerTriangular" | custom-call | tf_op jit(solution)/shard_map/jit(cholesky)/cholesky | solution.py:35
  372.6 0.2 convolution_dynamic-update-slice_fusion.1
  372.8 1.3 convolution_subtract_fusion.5
  374.2 11.7 %cholesky.255 = f32[128,128]{1,0:T(8,128)S(1)} custom-call(f32[128,128]{1,0:T(8,128)S(1)} %convolution_subtract_fusion.5), custom_call_target="Cholesky" | custom-call | tf_op jit(solution)/shard_map/jit(cholesky)/cholesky | solution.py:35
  385.9 0.7 compare_reduce_fusion.1
  386.6 0.6 compare_reduce_fusion
  387.3 0.7 compare_reduce_fusion.2
  390.5 1.3 select_select_fusion
  391.8 14.2 %while.1 = (s32[]{:T(128)}, f32[512,512]{1,0:T(8,128)}, s32[4,2]{0,1:T(2,128)S(1)}, f32[4,128,128]{2,1,0:T(8,128)}, s32[]{:T(128)}) while((s32[]{:T(128)}, f32[512,512]{1,0:T(8,128)}, s32[4,2]{0,1:T(2,128)S(1)}, f32[4,128,128]{2,1,0:T(8,128)}, s32[]{:T(128)}) %tuple.34), condition=%wide.while_cond, body=%wide.while_body.sunk | while | flops 2 | bytes 132205 | solution.py:36
  391.8 0.1 constant_dynamic-slice_fusion.2
  391.8 0.6 fusion.85
  392.4 2.9 bitcast_dynamic-update-slice_fusion.2
  395.3 0.1 constant_dynamic-slice_fusion.2
  395.4 0.6 fusion.85
  396.0 2.9 bitcast_dynamic-update-slice_fusion.2
  398.9 0.1 constant_dynamic-slice_fusion.2
  398.9 0.6 fusion.85
  399.5 2.9 bitcast_dynamic-update-slice_fusion.2
  402.4 0.1 constant_dynamic-slice_fusion.2
  402.5 0.6 fusion.85
  403.1 2.8 bitcast_dynamic-update-slice_fusion.2
  405.9 40.1 %custom-call.34 = f32[4,128,128]{1,2,0:T(8,128)S(1)} custom-call(f32[4,128,128]{2,1,0:T(8,128)} %get-tuple-element.10), custom_call_target="InvertDiagBlocksLowerTriangular" | custom-call | tf_op jit(solution)/shard_map/jit(_solve_triangular)/triangular_solve | solution.py:36
  446.0 0.3 fusion.43
  446.4 1.1 convolution_subtract_fusion.4
  447.5 0.3 fusion.50
  447.8 1.2 convolution_subtract_fusion.2
  449.0 0.3 fusion.48
  449.4 1.4 convolution_subtract_fusion.1
  450.7 0.3 fusion.47
  451.1 0.6 copy-done.6
  451.7 4.9 convolution_bitcast_fusion
  456.6 0.0 all-gather.3.cloned.1.call-start
  456.7 1.3 dynamic-slice.3
  458.6 167.0 %all-reduce.10.cloned.1.call-done = f32[1664,512]{0,1:T(8,128)} async-done(((f32[1664,512]{0,1:T(8,128)}), f32[1664,512]{0,1:T(8,128)}) %all-reduce.10.cloned.1.call-update) | async-done | bytes 3407888
  625.6 1.3 multiply_reduce_fusion
  626.9 0.8 copy.15
  628.4 101.2 %psum.23 = f32[512]{0:T(512)S(1)} all-reduce(f32[512]{0:T(512)S(1)} %get-tuple-element.27), channel_id=1, replica_groups=mesh['row'=32,'col'=16] {'row','col'}, use_global_device_ids=true, to_apply=%region_12.13 | all-reduce | flops 512 | bytes 4096 | tf_op jit(solution)/shard_map/psum | solution.py:52
  729.5 3.1 reshape.76
  732.7 8.7 %fusion.10 = f32[256,1664]{1,0:T(8,128)} fusion(f32[256,1664]{1,0:T(8,128)} %param.4, f32[1664,512]{1,0:T(8,128)S(1)} %reshape.76, f32[128,256]{1,0:T(8,128)} %copy-done.6, f32[128,256]{1,0:T(8,128)} %copy-done.4, f32[128,256]{1,0:T(8,128)} %copy-done.2, f32[128,256]{1,0:T(8,128)S(1)} %fusion.43), kind=kOutput, calls=%fused_computation.19 | convolution fusion | flops 2618490880 | bytes 7340032 | tf_op jit(solution)/shard_map/dot_general | solution.py:58
  741.4 0.4 broadcast_multiply_fusion
  741.8 1.7 copy-done
  743.5 0.3 dynamic-slice_bitcast_fusion
  743.8 0.9 copy.16
  744.8 9.1 %fusion.12 = bf16[256,1664]{1,0:T(8,128)(2,1)} fusion(f32[1664,512]{1,0:T(8,128)} %copy-done, bf16[256,1664]{1,0:T(8,128)(2,1)} %param.5, f32[]{:T(128)} %bitcast.16, f32[128,256]{1,0:T(8,128)} %copy-done.6, f32[128,256]{1,0:T(8,128)} %copy-done.4, f32[128,256]{1,0:T(8,128)} %copy-done.2, f32[128,256]{1,0:T(8,128)S(1)} %fusion.43), kind=kOutput, calls=%fused_computation.21 | convolution fusion | flops 2619342848 | bytes 5636100 | tf_op jit(solution)/shard_map/dot_general | solution.py:61
  (28 shorter events, 0.3 us)
Async XLA Ops:
  7.2 132.4 %all-reduce.6.cloned.1.call-start = ((), (), s32[]{:S(2)}) async-start(), calls=%async_computation | async-start | bytes 1048576 | tf_op jit(solution)/shard_map/psum | solution.py:45
  18.0 281.5 %all-reduce.8.cloned.1.call-start = ((), (), s32[]{:S(2)}) async-start(), calls=%async_computation.1 | async-start | bytes 2097152 | tf_op jit(solution)/shard_map/psum | solution.py:46
  142.8 482.9 %all-reduce.10.cloned.1.call-start = ((), (), s32[]{:S(2)}) async-start(), calls=%async_computation.3 | async-start | bytes 6815744
  302.5 1.0 copy-start.5
  315.4 130.6 %copy-start.3 = (f32[256,512]{0,1:T(8,128)S(1)}, f32[256,512]{0,1:T(8,128)}, u32[]{:S(2)}) copy-start(f32[256,512]{0,1:T(8,128)} %all-reduce.6.cloned.1.call-done) | copy-start | bytes 1572868
  372.6 79.1 %copy-start.1 = (f32[256,1664]{1,0:T(8,128)S(1)}, f32[256,1664]{1,0:T(8,128)}, u32[]{:S(2)}) copy-start(f32[256,1664]{1,0:T(8,128)} %param.4) | copy-start | bytes 5111812
  447.8 3.3 copy-start.2
  449.4 7.2 copy-start.4
  451.1 0.6 copy-start.6
  456.6 272.9 %all-gather.3.cloned.1.call-start = ((), (), s32[]{:S(2)}) async-start(), calls=%async_computation.2 | async-start | bytes 3784704 | tf_op jit(solution)/shard_map/all_gather | solution.py:54
  741.8 1.7 copy-start
Sparse Core Ops, SparseCore 0:
  18.2 121.3 all-reduce.5
  143.9 155.5 all-reduce.7
  456.7 168.8 all-reduce.9
  629.2 84.3 all-gather.2
where the time goes:
time: 768 us; the launch traced here: 761 us
  waiting for transfers between devices  445 us (58%)
  other arithmetic  123 us (16%)
  blocking collectives  101 us (13%)
  matrix products  46.6 us (6%)
  local copies, waits for them, and re-layouts  25.6 us (3%)
  between operations  19 us (2%)
    unnamed x5, waiting for transfers between devices  167 us
    psum x1, waiting for transfers between devices, per_device(): gram_matrix = lax.psum(inner_rows(projected, projected), 'row')  156 us
    psum x1, waiting for transfers between devices, per_device(): projected = lax.psum(partial_proj, 'col')  121 us
    psum x1, blocking collectives, per_device(): lax.psum(jnp.sum(right_share * right_share, axis=0), ('row', 'col'))  101 us
    another operation x14, other arithmetic, orthonormal(): factor_low = jnp.linalg.cholesky(gram_matrix)  78.6 us
    another operation x3, other arithmetic, orthonormal(): jax.scipy.linalg.solve_triangular(factor_low, projected.T, lower=True)  41.4 us
  transfers between devices with their start and end apart: 4, of which 3 were waited for; matrix products, arithmetic and copies ran while one was open for 0% of the time, Pallas kernels for 0%

commit v1 on v0

v1 whole, which is shorter than its diff:
```python
import functools

import jax
import jax.numpy as jnp
from jax import lax
from jax.experimental import pallas as pl
from jax.experimental.pallas import tpu as pltpu
from jax.sharding import PartitionSpec as P

ROWS = 8192
COLS = 26624
RANK = 512
MOMENTUM_DECAY = 0.95
EPSILON = 1e-06
NX, NY, NZ = 4, 8, 8
TR, TC = 256, 1664
WIDE = 1280
NARROW = TC - WIDE
XS = RANK // NX
SL = XS // NY
YS = RANK // NY
HALF = TR // 2
PZ = HALF // NZ
F32, BF16, I32 = jnp.float32, jnp.bfloat16, jnp.int32
MESH = pl.DeviceIdType.MESH
HIGHEST = lax.Precision.HIGHEST
NN = (((1,), (0,)), ((), ()))
NT = (((1,), (1,)), ((), ()))
TN = (((0,), (0,)), ((), ()))


def split(value):
    high = value.astype(BF16)
    return high, (value - high.astype(F32)).astype(BF16)


def dot(left, right, dims=NN):
    return lax.dot_general(left, right, dims, preferred_element_type=F32)


def dot3(left, right, dims=NN):
    return dot(left[0], right[0], dims) + (dot(left[0], right[1], dims) + dot(left[1], right[0], dims))


def exact(left, right, dims=NN):
    return lax.dot_general(left, right, dims, precision=HIGHEST, preferred_element_type=F32)


def eliminate(first, last, block):
    lane = lax.broadcasted_iota(I32, (128, 128), 1)
    row_at = lax.broadcasted_iota(I32, (128, 128), 0)
    lane_one = lax.broadcasted_iota(I32, (1, 128), 1)

    def group(index, a):
        live = row_at < 128 - 8 * index
        for s in range(8):
            pivot = a[s : s + 1, s : s + 1]
            root = lax.rsqrt(pivot)
            root = root * (1.5 - 0.5 * pivot * root * root)
            row = jnp.where(lane_one == s, root, a[s : s + 1, :] * root)
            below = live & (row_at > s)
            factor = jnp.where(below, a[:, s : s + 1] * root, 0.0)
            a = jnp.where(lane == s, 0.0, a) - factor * row
            a = jnp.where(row_at == s, row, a)
        a = pltpu.roll(a, 120, 1)
        return jnp.concatenate([a[8:], a[:8]], axis=0)

    return lax.fori_loop(first, last, group, block)


def communicate(mom, seed, q_out, r_out, s_out, mh, ml, vh, vl, pp, ch, ph, zr, pf, pt, gp, gx, g1, gy, gs, gram, wp, xr, yr, bx, by, wt, acc,
                sq, sqr, sqc, sems_s, sems_r):
    r, c = lax.axis_index("row"), lax.axis_index("col")
    y, x, z, k = r // NX, r % NX, c // 2, c % 2
    used = [0]
    pending = []

    def peer(dx=0, dy=0, dz=0, dk=0):
        return (lax.rem(y + dy, NY) * NX + lax.rem(x + dx, NX), lax.rem(z + dz, NZ) * 2 + lax.rem(k + dk, 2))

    def send(src, dst, **where):
        slot = used[0]
        used[0] += 1
        copy = pltpu.make_async_remote_copy(
            src_ref=src, dst_ref=dst, send_sem=sems_s.at[slot], recv_sem=sems_r.at[slot], device_id=peer(**where), device_id_type=MESH
        )
        copy.start()
        pending.append(copy)
        return copy

    def sent(copy):
        copy.wait_send()
        pending[:] = [other for other in pending if other is not copy]

    xd, yd, zd = range(1, NX), range(1, NY), range(1, NZ)
    barrier = pltpu.get_barrier_semaphore()
    others = [dict(dk=1)] + [dict(dx=d) for d in xd] + [dict(dy=d) for d in yd] + [dict(dz=d) for d in zd]
    for where in others:
        pl.semaphore_signal(barrier, inc=1, device_id=peer(**where), device_id_type=MESH)

    rank_at = lax.broadcasted_iota(I32, (128, RANK), 0) * RANK + lax.broadcasted_iota(I32, (128, RANK), 1)
    base = rank_at * 747796405 + (seed[0] * 277803737 + 1013904223)

    @pl.loop(0, TC // 128)
    def _(part):
        mixed = base + (c * TC + part * 128) * (RANK * 747796405 % 2**32 - 2**32 * (RANK * 747796405 % 2**32 >= 2**31))
        mixed = jnp.bitwise_xor(mixed, jnp.right_shift(mixed, 15))
        mixed = mixed * 1664525
        mixed = jnp.bitwise_xor(mixed, jnp.right_shift(mixed, 13))
        value = jnp.bitwise_and(mixed, 65535).astype(F32) * (1.0 / 32768.0) - 1.0
        high, low = split(value)
        here = pl.ds(pl.multiple_of(part * 128, 128), 128)
        vh[here, :] = high
        vl[here, :] = low
        high, low = split(mom[:, here])
        mh[:, here] = high
        ml[:, here] = low

    for half in range(2):
        rows = slice(half * HALF, (half + 1) * HALF)
        pp[rows, :] = dot3((mh[rows, :], ml[rows, :]), (vh[...], vl[...]))
    pl.semaphore_wait(barrier, len(others))

    mine = pl.ds(pl.multiple_of(k * HALF, HALF), HALF)
    send(pp.at[pl.ds(pl.multiple_of((1 - k) * HALF, HALF), HALF)], ch, dk=1).wait_recv()
    ph[...] = pp[mine, :] + ch[...]
    copies = [send(ph.at[pl.ds(pl.multiple_of(lax.rem(z + d, NZ) * PZ, PZ), PZ)], zr.at[d - 1], dz=d) for d in zd]
    for copy in copies:
        copy.wait_recv()
    total = ph[pl.ds(pl.multiple_of(z * PZ, PZ), PZ), :]
    for d in zd:
        total = total + zr[d - 1]

    def p_rows(core, dz):
        return pl.ds(pl.multiple_of(core * HALF + lax.rem(z + dz, NZ) * PZ, PZ), PZ)

    pf[p_rows(k, 0), :] = total
    copies = [send(pf.at[p_rows(k, 0)], pf.at[p_rows(k, 0)], dz=d) for d in zd]
    siblings = [send(pf.at[p_rows(k, 0)], pf.at[p_rows(k, 0)], dk=1)]
    for d in zd:
        copies[d - 1].wait_recv()
        siblings.append(send(pf.at[p_rows(k, NZ - d)], pf.at[p_rows(k, NZ - d)], dk=1))
    for copy in siblings:
        copy.wait_recv()

    pt[...] = pf[...].T
    spot = k * 64 + z * 8
    for i in range(NX):
        gp[i * 8 : (i + 1) * 8, :] = pt[pl.ds(pl.multiple_of(i * XS + spot, 8), 8), :]
    gp2 = exact(gp[...], pf[...])
    gx[0] = gp2
    gcopies = [send(gx.at[0, pl.ds(pl.multiple_of(lax.rem(x + d, NX) * 8, 8), 8)], gx.at[d, pl.ds(0, 8)], dx=d) for d in xd]

    for i in range(NX):
        here = pl.ds(pl.multiple_of(i * XS, XS), XS)
        wp[here, :] = dot3(split(pt[here, :]), (mh[...], ml[...]))

    for copy in gcopies:
        copy.wait_recv()
    total = gx[0, pl.ds(pl.multiple_of(x * 8, 8), 8), :]
    for d in xd:
        total = total + gx[d, 0:8, :]
    g1[...] = total
    gcopies = [send(g1, gy.at[d - 1], dy=d) for d in yd]

    def a_rows(dx, dy):
        return pl.ds(pl.multiple_of(lax.rem(x + dx, NX) * XS + lax.rem(y + dy, NY) * SL, SL), SL)

    wide, narrow = pl.ds(0, WIDE), pl.ds(WIDE, NARROW)
    order = list(yd) + [0]
    xcopies = {}
    for e in order:
        for d in xd:
            xcopies[e, d] = send(wp.at[a_rows(d, e), wide], xr.at[d - 1, e], dx=d)

    def b_block(dy):
        return pl.ds(pl.multiple_of(lax.rem(y + dy, NY) * YS, YS), YS)

    for copy in gcopies:
        copy.wait_recv()
    total = g1[...]
    for d in yd:
        total = total + gy[d - 1]
    gs[pl.ds(pl.multiple_of(x * 8, 8), 8), :] = total
    own = pl.ds(pl.multiple_of(x * 8, 8), 8)
    gcopies = [send(gs.at[own], gs.at[own], dx=d) for d in xd]
    bcopies = [send(wp.at[b_block(d), narrow], by.at[d - 1], dy=d) for d in yd]
    for copy in gcopies:
        copy.wait_recv()

    def g_rows(i, core, dz):
        return pl.ds(pl.multiple_of(i * XS + core * 64 + lax.rem(z + dz, NZ) * 8, 8), 8)

    for i in range(NX):
        gram[g_rows(i, k, 0), :] = gs[i * 8 : (i + 1) * 8, :]
    zcopies = {}
    for i in range(NX):
        right = pl.ds(i * XS, RANK - i * XS)
        for d in zd:
            zcopies[i, d] = send(gram.at[g_rows(i, k, 0), right], gram.at[g_rows(i, k, 0), right], dz=d)
    scopies = []
    for i in range(NX):
        right = pl.ds(i * XS, RANK - i * XS)
        for d in zd:
            zcopies[i, d].wait_recv()
        rows = pl.ds(pl.multiple_of(i * XS + k * 64, 64), 64)
        scopies.append(send(gram.at[rows, right], gram.at[rows, right], dk=1))

    def wide_first(es):
        for e in es:
            for d in xd:
                xcopies[e, d].wait_recv()
            rows = a_rows(0, e)
            total = wp[rows, wide]
            for d in xd:
                total = total + xr[d - 1, e]
            wp[rows, wide] = total
            if e:
                ycopies[e] = send(wp.at[rows, wide], yr.at[e - 1], dy=e)

    def wide_second():
        for e in yd:
            ycopies[e].wait_recv()
        rows = a_rows(0, 0)
        total = wp[rows, wide]
        for e in yd:
            total = total + yr[e - 1]
        wt[rows, wide] = total
        for e in yd:
            agy[e] = send(wt.at[rows, wide], wt.at[rows, wide], dy=e)
        for d in xd:
            agx.append(send(wt.at[rows, wide], wt.at[rows, wide], dx=d))

    def wide_third(es):
        for e in es:
            agy[e].wait_recv()
            rows = a_rows(0, NY - e)
            for d in xd:
                agx.append(send(wt.at[rows, wide], wt.at[rows, wide], dx=d))

    def b_rows(dx):
        return pl.ds(pl.multiple_of(y * YS + lax.rem(x + dx, NX) * SL, SL), SL)

    def narrow_first():
        for copy in bcopies:
            copy.wait_recv()
        rows = b_block(0)
        total = wp[rows, narrow]
        for e in yd:
            total = total + by[e - 1]
        wp[rows, narrow] = total
        for d in xd:
            bxc.append(send(wp.at[b_rows(d), narrow], bx.at[d - 1], dx=d))

    def narrow_second():
        for copy in bxc:
            copy.wait_recv()
        rows = b_rows(0)
        total = wp[rows, narrow]
        for d in xd:
            total = total + bx[d - 1]
        wt[rows, narrow] = total
        for d in xd:
            bgx.append(send(wt.at[rows, narrow], wt.at[rows, narrow], dx=d))

    def narrow_third():
        for copy in bgx:
            copy.wait_recv()
        for e in yd:
            bgy.append(send(wt.at[b_block(0), narrow], wt.at[b_block(0), narrow], dy=e))

    ycopies, agy, agx, bxc, bgx, bgy = {}, {}, [], [], [], []
    between = [
        lambda: wide_first((1, 2, 3)),
        lambda: (wide_first((4, 5, 6, 7, 0)), narrow_first()),
        lambda: narrow_second(),
        lambda: (wide_second(), narrow_third()),
        lambda: wide_third((1, 7, 2)),
        lambda: wide_third((6, 3, 5)),
        lambda: wide_third((4,)),
        lambda: None,
    ]

    scopies[0].wait_recv()

    for b in range(NX):
        low, high = b * XS, (b + 1) * XS
        block = eliminate(0, 8, gram[low:high, low:high])
        between[2 * b]()
        block = eliminate(8, 16, block)
        between[2 * b + 1]()
        if b == 0:
            for copy in scopies[1:]:
                copy.wait_recv()
            for copy in list(zcopies.values()) + scopies:
                sent(copy)
        panel = exact(block, gram[low:high, :])
        gram[low:high, :] = panel
        gram[low:high, low:high] = block
        if b < NX - 1:
            factor = gram[low:high, high:].T
            cross = exact(factor, gram[low:high, :])
            old = gram[high:, :]
            spot_lane = lax.broadcasted_iota(I32, (RANK - high, RANK), 1)
            gram[high:, :] = jnp.where((spot_lane >= low) & (spot_lane < high), 0.0, old) - cross

    inverse = gram
    q_in = split(pf[...])
    for b in range(NX):
        high = (b + 1) * XS
        q_out[:, b * XS : high] = dot3((q_in[0][:, :high], q_in[1][:, :high]), split(inverse[b * XS : high, :high]), NT)

    for copy in agx + bgy:
        copy.wait_recv()
    factors = [split(inverse[b * XS : (b + 1) * XS, : (b + 1) * XS]) for b in range(NX)]
    acc[...] = jnp.zeros_like(acc)

    @pl.loop(0, TC // 128)
    def _(part):
        here = pl.ds(pl.multiple_of(part * 128, 128), 128)
        high, low = split(wt[:, here])
        for b in range(NX):
            end = (b + 1) * XS
            rows = slice(b * XS, end)
            piece = dot3(factors[b], (high[:end], low[:end]))
            r_out[rows, here] = piece
            acc[rows, :] += piece * piece

    sub = lax.broadcasted_iota(I32, (8, 128), 0)
    packed = jnp.zeros((8, 128), F32)
    for b in range(NX):
        packed = jnp.where(sub == b, exact(jnp.ones((8, 128), F32), acc[b * XS : (b + 1) * XS, :], NT), packed)
    sq[...] = packed
    copies = [send(sq, sqr.at[d - 1], dz=d) for d in zd]
    for copy in copies:
        copy.wait_recv()
    for d in zd:
        packed = packed + sqr[d - 1]
    sqc[0] = packed
    send(sqc.at[0], sqc.at[1], dk=1).wait_recv()
    s_out[...] = lax.rsqrt((sqc[0] + sqc[1]) * (1.0 / COLS) + EPSILON)
    for copy in pending:
        copy.wait_send()


SENDS = 1 + 7 + 7 + 8 + 3 + 7 + 24 + 3 + 7 + 28 + 4 + 7 + 7 + 24 + 3 + 3 + 7 + 7 + 1


def outputs(mom, weight, q, r, s, rate, mom_out, weight_out):
    sub = lax.broadcasted_iota(I32, (8, 128), 0)
    scales = jnp.concatenate([jnp.sum(jnp.where(sub == b, s[...], 0.0), axis=0, keepdims=True) for b in range(NX)], axis=1)
    basis = q[...]
    right = split(r[...])
    feedback = dot(basis.astype(BF16), right[0])
    update = dot3(split(basis * scales), right) * (ROWS / RANK) ** 0.5
    mom_out[...] = mom[...] - (1.0 - MOMENTUM_DECAY) * feedback
    weight_out[...] = (weight[...].astype(F32) - rate[0] * update).astype(BF16)


def per_device(momentum, weight, init_seed, step_rate):
    vmem, smem = pl.BlockSpec(memory_space=pltpu.VMEM), pl.BlockSpec(memory_space=pltpu.SMEM)
    q, right, scales = pl.pallas_call(
        communicate,
        out_shape=[jax.ShapeDtypeStruct((TR, RANK), F32), jax.ShapeDtypeStruct((RANK, TC), F32), jax.ShapeDtypeStruct((8, 128), F32)],
        in_specs=[vmem, smem],
        out_specs=[vmem, vmem, vmem],
        scratch_shapes=[
            pltpu.VMEM((TR, TC), BF16),
            pltpu.VMEM((TR, TC), BF16),
            pltpu.VMEM((TC, RANK), BF16),
            pltpu.VMEM((TC, RANK), BF16),
            pltpu.VMEM((TR, RANK), F32),
            pltpu.VMEM((HALF, RANK), F32),
            pltpu.VMEM((HALF, RANK), F32),
            pltpu.VMEM((NZ - 1, PZ, RANK), F32),
            pltpu.VMEM((TR, RANK), F32),
            pltpu.VMEM((RANK, TR), F32),
            pltpu.VMEM((32, TR), F32),
            pltpu.VMEM((NX, 32, RANK), F32),
            pltpu.VMEM((8, RANK), F32),
            pltpu.VMEM((NY - 1, 8, RANK), F32),
            pltpu.VMEM((32, RANK), F32),
            pltpu.VMEM((RANK, RANK), F32),
            pltpu.VMEM((RANK, TC), F32),
            pltpu.VMEM((NX - 1, NY, SL, WIDE), F32),
            pltpu.VMEM((NY - 1, SL, WIDE), F32),
            pltpu.VMEM((NX - 1, SL, NARROW), F32),
            pltpu.VMEM((NY - 1, YS, NARROW), F32),
            pltpu.VMEM((RANK, TC), F32),
            pltpu.VMEM((RANK, 128), F32),
            pltpu.VMEM((8, 128), F32),
            pltpu.VMEM((NZ - 1, 8, 128), F32),
            pltpu.VMEM((2, 8, 128), F32),
            pltpu.SemaphoreType.DMA((SENDS,)),
            pltpu.SemaphoreType.DMA((SENDS,)),
        ],
        compiler_params=pltpu.CompilerParams(collective_id=0, has_side_effects=True, vmem_limit_bytes=56 * 2**20),
        name="communicate",
    )(momentum, init_seed)
    tile = pl.BlockSpec((TR, 128), lambda i: (0, i))
    momentum_next, weight_next = pl.pallas_call(
        outputs,
        grid=(TC // 128,),
        out_shape=[jax.ShapeDtypeStruct((TR, TC), F32), jax.ShapeDtypeStruct((TR, TC), BF16)],
        in_specs=[
            tile,
            tile,
            pl.BlockSpec((TR, RANK), lambda i: (0, 0)),
            pl.BlockSpec((RANK, 128), lambda i: (0, i)),
            pl.BlockSpec((8, 128), lambda i: (0, 0)),
            smem,
        ],
        out_specs=[tile, tile],
        compiler_params=pltpu.CompilerParams(vmem_limit_bytes=40 * 2**20),
        name="outputs",
    )(momentum, weight, q, right, scales, step_rate)
    begin = lax.axis_index("row") * SL
    scale_here = lax.dynamic_slice_in_dim(scales[:NX].reshape(RANK), begin, SL, 0)
    next_factor = lax.dynamic_slice_in_dim(right, begin, SL, 0) * scale_here[:, None]
    return (momentum_next, weight_next, next_factor)


def solution(mesh):
    placed = (P("row", "col"), P("row", "col"), P(), P())
    return jax.shard_map(
        per_device,
        mesh=mesh,
        in_specs=placed,
        out_specs=(P("row", "col"), P("row", "col"), P("row", "col")),
        check_vma=False,
    )
```

time: 768 us -> 186 us (0.24)
  waiting for transfers between devices: 445 us -> 0 us
  Pallas kernels: 0 us -> 173 us
  other arithmetic: 123 us -> 1.61 us
  blocking collectives: 101 us -> 0 us
  matrix products: 46.6 us -> 0 us
  local copies, waits for them, and re-layouts: 25.6 us -> 6.37 us
  between operations: 19 us -> 1.95 us
    psum x2 -> x0, waiting for transfers between devices: 278 us -> none  [the longest x1 156 us: per_device(): gram_matrix = lax.psum(inner_rows(projected, projected), 'row')]
    pallas_call x0 -> x2, Pallas kernels: none -> 173 us  [the longest x1 165 us: per_device(): pl.pallas_call(communicate, out_shape=[jax.ShapeDtypeStruct((TR, RANK), F...]
    unnamed x5 -> x0, waiting for transfers between devices: 167 us -> none
    another operation x17 -> x0, other arithmetic: 120 us -> none  [the longest x14 78.6 us: orthonormal(): factor_low = jnp.linalg.cholesky(gram_matrix)]
    psum x1 -> x0, blocking collectives: 101 us -> none  [per_device(): lax.psum(jnp.sum(right_share * right_share, axis=0), ('row', 'col'))]
    dot_general x5 -> x0, matrix products: 36.1 us -> none  [the longest x1 10.1 us: per_device(): partial_proj = jnp.dot(momentum, start_factor, precision=HIGHEST)]
    another operation x17 -> x0, local copies, waits for them, and re-layouts: 14.3 us -> none
    another operation x13 -> x0, matrix products: 10.5 us -> none  [the longest x6 5.58 us: orthonormal(): factor_low = jnp.linalg.cholesky(gram_matrix)]
  transfers between devices with their start and end apart: 4 -> 0, of which waited for: 3 -> 0; matrix products, arithmetic and copies ran while one was open for 0% -> 0% of each run, Pallas kernels for 0% -> 0%
where the time goes in v1:
time: 186 us; the launch traced here: 183 us
  Pallas kernels  173 us (93%)
  local copies, waits for them, and re-layouts  6.37 us (3%)
  between operations  1.95 us (1%)
    pallas_call x1, Pallas kernels, per_device(): pl.pallas_call(communicate, out_shape=[jax.ShapeDtypeStruct((TR, RANK), F...  165 us
    pallas_call x1, Pallas kernels, per_device(): pl.pallas_call(outputs, grid=(TC // 128,), out_shape=[jax.ShapeDtypeStruc...  7.87 us
    unnamed x12, local copies, waits for them, and re-layouts  6.29 us

profile of v1, /device:TPU:1, one launch (start us, length us, event | category | flops | bytes accessed | tf_op | source)
XLA Modules:
  0.0 183.0 jit_solution(12607004066039847609)
XLA Ops:
  1.3 165.2 %communicate.1 = (f32[256,512]{1,0:T(8,128)}, f32[512,1664]{1,0:T(8,128)}, f32[8,128]{1,0:T(8,128)}) custom-call(f32[256,1664]{1,0:T(8,128)} %mom.3, s32[1]{0:T(128)S(6)} %copy.7.seed), custom_call_target="tpu_custom_call" | custom-call | tf_op jit(solution)/shard_map/communicate/pallas_call | solution.py:362
  166.4 0.0 copy-start.5
  167.1 0.0 copy-start
  167.1 1.4 copy-done
  168.6 0.0 copy-start.1
  168.6 2.0 %copy-done.1 = f32[512,1664]{1,0:T(8,128)S(1)} copy-done((f32[512,1664]{1,0:T(8,128)S(1)}, f32[512,1664]{1,0:T(8,128)}, u32[]{:S(2)}) %copy-start.1) | copy-done | bytes 3407896
  170.5 0.0 copy-start.2
  170.5 1.2 copy-done.2
  171.7 0.0 copy-start.3
  171.7 1.0 copy-done.3
  172.7 0.0 copy-start.4
  172.7 0.7 copy-done.4
  173.4 7.9 %outputs.1 = (f32[256,1664]{1,0:T(8,128)}, bf16[256,1664]{1,0:T(8,128)(2,1)}) custom-call(f32[256,1664]{1,0:T(8,128)S(1)} %copy-done, bf16[256,1664]{1,0:T(8,128)(2,1)S(1)} %copy-done.2, f32[256,512]{1,0:T(8,128)S(1)} %copy-done.3, f32[512,1664]{1,0:T(8,128)S(1)} %copy-done.1, f32[8,128]{1,0:T(8,128)S(1)} %copy-done.4, f32[1]{0:T(128)S(6)} %copy.8.rate), custom_call_target="tpu_custom_call" | custom-call | tf_op jit(solution)/shard_map/outputs/pallas_call | solution.py:401
  181.3 0.0 copy-done.5
  181.3 0.1 dynamic_slice.7
  181.3 1.6 dynamic-slice_multiply_fusion
  (1 shorter events, 0.0 us)
Async XLA Ops:
  166.4 14.8 %copy-start.5 = (f32[8,128]{1,0:T(8,128)S(1)}, f32[8,128]{1,0:T(8,128)}, u32[]{:S(2)}) copy-start(f32[8,128]{1,0:T(8,128)} %get-tuple-element.10.s) | copy-start | bytes 12292
  167.1 1.5 copy-start
  168.6 2.0 %copy-start.1 = (f32[512,1664]{1,0:T(8,128)S(1)}, f32[512,1664]{1,0:T(8,128)}, u32[]{:S(2)}) copy-start(f32[512,1664]{1,0:T(8,128)} %get-tuple-element.9.r) | copy-start | bytes 10223620
  170.5 1.2 copy-start.2
  171.7 1.0 copy-start.3
  172.7 0.7 copy-start.4

commit v2 on v1

v2 whole, which is shorter than its diff:
```python
import functools

import jax
import jax.numpy as jnp
from jax import lax
from jax.experimental import pallas as pl
from jax.experimental.pallas import tpu as pltpu
from jax.sharding import PartitionSpec as P

ROWS = 8192
COLS = 26624
RANK = 512
MOMENTUM_DECAY = 0.95
EPSILON = 1e-06
NX, NY, NZ = 4, 8, 8
TR, TC = 256, 1664
WIDE = 1024
NARROW = TC - WIDE
LEFT = 384
XS = RANK // NX
SL = XS // NY
YS = RANK // NY
HALF = TR // 2
PARTS = ((0, 512), (512, 512), (1024, 640))
PZ = HALF // NZ
F32, BF16, I32 = jnp.float32, jnp.bfloat16, jnp.int32
MESH = pl.DeviceIdType.MESH
HIGHEST = lax.Precision.HIGHEST
NN = (((1,), (0,)), ((), ()))
NT = (((1,), (1,)), ((), ()))
TN = (((0,), (0,)), ((), ()))


def split(value):
    high = value.astype(BF16)
    return high, (value - high.astype(F32)).astype(BF16)


def dot(left, right, dims=NN):
    return lax.dot_general(left, right, dims, preferred_element_type=F32)


def dot3(left, right, dims=NN):
    return dot(left[0], right[0], dims) + (dot(left[0], right[1], dims) + dot(left[1], right[0], dims))


def exact(left, right, dims=NN):
    return lax.dot_general(left, right, dims, precision=HIGHEST, preferred_element_type=F32)


def eliminate(tiles, groups):
    lane = lax.broadcasted_iota(I32, (8, 128), 1)
    sub = lax.broadcasted_iota(I32, (8, 128), 0)

    def spread(value):
        return jnp.broadcast_to(value, (8, 128))

    for q in groups:
        o = 8 * q
        top = tiles[q]
        columns = [spread(top[:, o + s : o + s + 1]) for s in range(8)]
        item = {(s, t): spread(columns[s][t : t + 1, :]) for s in range(8) for t in range(s, 8)}
        rows = [spread(top[s : s + 1, :]) for s in range(8)]
        lower, roots, done = {}, [], []
        for s in range(8):
            root = lax.rsqrt(item[s, s])
            roots.append(root)
            for t in range(s + 1, 8):
                lower[t, s] = item[s, t] * root
            for t in range(s + 1, 8):
                for u in range(t, 8):
                    item[t, u] = item[t, u] - lower[t, s] * lower[u, s]
            full = jnp.where(lane == o + s, root, rows[s] * root)
            for t in range(s + 1, 8):
                rows[t] = jnp.where(lane == o + s, 0.0, rows[t]) - lower[t, s] * full
            done.append(jnp.where((lane > o + s) & (lane < o + 8), 0.0, full))
        new = done[0]
        for s in range(1, 8):
            new = jnp.where(sub == s, done[s], new)
        tiles[q] = new
        here = (lane >= o) & (lane < o + 8)
        for i in range(16):
            if i < q:
                tiles[i] = jnp.where(here, 0.0, tiles[i])
            if i > q:
                rest = jnp.where(here, 0.0, tiles[i])
                factors = []
                for s in range(8):
                    factor = spread(tiles[i][:, o + s : o + s + 1])
                    for u in range(s):
                        factor = factor - factors[u] * lower[s, u]
                    factor = factor * roots[s]
                    factors.append(factor)
                    rest = rest - factor * done[s]
                tiles[i] = rest


def update_tile(mom, weight_in, seed, rate, mom_out, weight_out, next_out, w_in, mom_new, w_new, next_new, qb, rt, rh, rl, mh, ml, vh, vl, pp, ch, ph, zr, pf, pt, gp, gx, g1, gy, gs, gram, wp, xr, yr, bx, by, wt,
                sq, sqr, sqc, sems_s, sems_r, sems_l):
    r, c = lax.axis_index("row"), lax.axis_index("col")
    y, x, z, k = r // NX, r % NX, c // 2, c % 2
    used = [0]
    pending = []

    def peer(dx=0, dy=0, dz=0, dk=0):
        return (lax.rem(y + dy, NY) * NX + lax.rem(x + dx, NX), lax.rem(z + dz, NZ) * 2 + lax.rem(k + dk, 2))

    def send(src, dst, **where):
        slot = used[0]
        used[0] += 1
        copy = pltpu.make_async_remote_copy(
            src_ref=src, dst_ref=dst, send_sem=sems_s.at[slot], recv_sem=sems_r.at[slot], device_id=peer(**where), device_id_type=MESH
        )
        copy.start()
        pending.append(copy)
        return copy

    def sent(copy):
        copy.wait_send()
        pending[:] = [other for other in pending if other is not copy]

    xd, yd, zd = range(1, NX), range(1, NY), range(1, NZ)
    barrier = pltpu.get_barrier_semaphore()
    others = [dict(dk=1)] + [dict(dx=d) for d in xd] + [dict(dy=d) for d in yd] + [dict(dz=d) for d in zd]
    for where in others:
        pl.semaphore_signal(barrier, inc=1, device_id=peer(**where), device_id_type=MESH)

    weight_copy = pltpu.make_async_copy(weight_in, w_in, sems_l.at[0])
    weight_copy.start()

    rank_at = lax.broadcasted_iota(I32, (128, RANK), 0) * RANK + lax.broadcasted_iota(I32, (128, RANK), 1)
    base = rank_at * 747796405 + (seed[0] * 277803737 + 1013904223)

    @pl.loop(0, TC // 128)
    def _(part):
        mixed = base + (c * TC + part * 128) * (RANK * 747796405 % 2**32 - 2**32 * (RANK * 747796405 % 2**32 >= 2**31))
        mixed = jnp.bitwise_xor(mixed, jnp.right_shift(mixed, 15))
        mixed = mixed * 1664525
        mixed = jnp.bitwise_xor(mixed, jnp.right_shift(mixed, 13))
        value = jnp.bitwise_and(mixed, 65535).astype(F32) * (1.0 / 32768.0) - 1.0
        high, low = split(value)
        here = pl.ds(pl.multiple_of(part * 128, 128), 128)
        vh[here, :] = high
        vl[here, :] = low
        high, low = split(mom[:, here])
        mh[:, here] = high
        ml[:, here] = low

    for half in range(2):
        rows = slice(half * HALF, (half + 1) * HALF)
        pp[rows, :] = dot3((mh[rows, :], ml[rows, :]), (vh[...], vl[...]))
    pl.semaphore_wait(barrier, len(others))

    mine = pl.ds(pl.multiple_of(k * HALF, HALF), HALF)
    send(pp.at[pl.ds(pl.multiple_of((1 - k) * HALF, HALF), HALF)], ch, dk=1).wait_recv()
    ph[...] = pp[mine, :] + ch[...]
    copies = [send(ph.at[pl.ds(pl.multiple_of(lax.rem(z + d, NZ) * PZ, PZ), PZ)], zr.at[d - 1], dz=d) for d in zd]
    for copy in copies:
        copy.wait_recv()
    total = ph[pl.ds(pl.multiple_of(z * PZ, PZ), PZ), :]
    for d in zd:
        total = total + zr[d - 1]

    def p_rows(core, dz):
        return pl.ds(pl.multiple_of(core * HALF + lax.rem(z + dz, NZ) * PZ, PZ), PZ)

    pf[p_rows(k, 0), :] = total
    copies = [send(pf.at[p_rows(k, 0)], pf.at[p_rows(k, 0)], dz=d) for d in zd]
    siblings = [send(pf.at[p_rows(k, 0)], pf.at[p_rows(k, 0)], dk=1)]
    for d in zd:
        copies[d - 1].wait_recv()
        siblings.append(send(pf.at[p_rows(k, NZ - d)], pf.at[p_rows(k, NZ - d)], dk=1))
    for copy in siblings:
        copy.wait_recv()

    pt[...] = pf[...].T
    spot = k * 64 + z * 8
    for i in range(NX):
        gp[i * 8 : (i + 1) * 8, :] = pt[pl.ds(pl.multiple_of(i * XS + spot, 8), 8), :]
    gp2 = exact(gp[...], pf[...])
    gx[0] = gp2
    gcopies = [send(gx.at[0, pl.ds(pl.multiple_of(lax.rem(x + d, NX) * 8, 8), 8)], gx.at[d, pl.ds(0, 8)], dx=d) for d in xd]

    for i in range(NX):
        here = pl.ds(pl.multiple_of(i * XS, XS), XS)
        wp[here, :] = dot3(split(pt[here, :]), (mh[...], ml[...]))

    wide, narrow = pl.ds(0, WIDE), pl.ds(WIDE, NARROW)
    left, right_half = pl.ds(WIDE, LEFT), pl.ds(WIDE + LEFT, NARROW - LEFT)

    def a_rows(dx, dy):
        return pl.ds(pl.multiple_of(lax.rem(x + dx, NX) * XS + lax.rem(y + dy, NY) * SL, SL), SL)

    def b_block(dy):
        return pl.ds(pl.multiple_of(lax.rem(y + dy, NY) * YS, YS), YS)

    def b_rows(dx):
        return pl.ds(pl.multiple_of(y * YS + lax.rem(x + dx, NX) * SL, SL), SL)

    xcopies, ycopies, agy, agx, bup, bdown, bxc, bgx, bgup, bgdown = {}, {}, {}, [], {}, {}, [], [], {}, {}

    def wide_start(es):
        for e in es:
            for d in xd:
                xcopies[e, d] = send(wp.at[a_rows(d, e), wide], xr.at[d - 1, e], dx=d)

    def wide_first(e):
        for d in xd:
            xcopies[e, d].wait_recv()
        rows = a_rows(0, e)
        total = wp[rows, wide]
        for d in xd:
            total = total + xr[d - 1, e]
        wp[rows, wide] = total
        if e:
            ycopies[e] = send(wp.at[rows, wide], yr.at[e - 1], dy=e)

    def wide_second():
        for e in yd:
            ycopies[e].wait_recv()
        rows = a_rows(0, 0)
        total = wp[rows, wide]
        for e in yd:
            total = total + yr[e - 1]
        wt[rows, wide] = total
        for d in xd:
            agx.append(send(wt.at[rows, wide], wt.at[rows, wide], dx=d))
        for e in (1, 7, 2, 6, 3, 5, 4):
            agy[e] = send(wt.at[rows, wide], wt.at[rows, wide], dy=e)

    def wide_third(e):
        agy[e].wait_recv()
        rows = a_rows(0, NY - e)
        for d in xd:
            agx.append(send(wt.at[rows, wide], wt.at[rows, wide], dx=d))

    def narrow_start():
        bup[4] = send(wp.at[b_block(4), left], by.at[0, :, pl.ds(0, LEFT)], dy=1)
        bdown[4] = send(wp.at[b_block(4), right_half], by.at[4, :, pl.ds(LEFT, NARROW - LEFT)], dy=NY - 1)

    def narrow_step(d):
        bup[d + 1].wait_recv()
        bdown[d + 1].wait_recv()
        if d == 3:
            wp[b_block(3), left] += by[0, :, 0:LEFT]
            wp[b_block(5), right_half] += by[4, :, LEFT:NARROW]
        else:
            wp[b_block(d), narrow] += by[3 - d]
            wp[b_block(NY - d), narrow] += by[7 - d]
        bup[d] = send(wp.at[b_block(d), narrow], by.at[4 - d], dy=1)
        bdown[d] = send(wp.at[b_block(NY - d), narrow], by.at[8 - d], dy=NY - 1)

    def narrow_first():
        bup[1].wait_recv()
        bdown[1].wait_recv()
        wp[b_block(0), narrow] += by[3] + by[7]
        for d in xd:
            bxc.append(send(wp.at[b_rows(d), narrow], bx.at[d - 1], dx=d))

    def narrow_second():
        for copy in bxc:
            copy.wait_recv()
        rows = b_rows(0)
        total = wp[rows, narrow]
        for d in xd:
            total = total + bx[d - 1]
        wt[rows, narrow] = total
        for d in xd:
            bgx.append(send(wt.at[rows, narrow], wt.at[rows, narrow], dx=d))

    def narrow_gather(d):
        if d == 0:
            for copy in bgx:
                copy.wait_recv()
        else:
            bgup[d - 1].wait_recv()
            bgdown[d - 1].wait_recv()
        up, down = (left, right_half) if d == 3 else (narrow, narrow)
        bgup[d] = send(wt.at[b_block(NY - d if d else 0), up], wt.at[b_block(NY - d if d else 0), up], dy=1)
        bgdown[d] = send(wt.at[b_block(d), down], wt.at[b_block(d), down], dy=NY - 1)

    for copy in gcopies:
        copy.wait_recv()
    total = gx[0, pl.ds(pl.multiple_of(x * 8, 8), 8), :]
    for d in xd:
        total = total + gx[d, 0:8, :]
    g1[...] = total
    gcopies = [send(g1, gy.at[d - 1], dy=d) for d in yd]
    wide_start((1, 2, 3))
    narrow_start()
    for copy in gcopies:
        copy.wait_recv()
    total = g1[...]
    for d in yd:
        total = total + gy[d - 1]
    own = pl.ds(pl.multiple_of(x * 8, 8), 8)
    gs[own, :] = total
    gcopies = [send(gs.at[own], gs.at[own], dx=d) for d in xd]
    wide_start((4, 5, 6, 7, 0))
    narrow_step(3)
    wide_first(1)
    for copy in gcopies:
        copy.wait_recv()

    def g_rows(i, core, dz):
        return pl.ds(pl.multiple_of(i * XS + core * 64 + lax.rem(z + dz, NZ) * 8, 8), 8)

    for i in range(NX):
        gram[g_rows(i, k, 0), :] = gs[i * 8 : (i + 1) * 8, :]
    zcopies = {}
    for i in range(NX):
        right = pl.ds(i * XS, RANK - i * XS)
        for d in zd:
            zcopies[i, d] = send(gram.at[g_rows(i, k, 0), right], gram.at[g_rows(i, k, 0), right], dz=d)
    wide_first(2)
    narrow_step(2)
    wide_first(3)
    scopies = []
    for i in range(NX):
        right = pl.ds(i * XS, RANK - i * XS)
        for d in zd:
            zcopies[i, d].wait_recv()
        rows = pl.ds(pl.multiple_of(i * XS + k * 64, 64), 64)
        scopies.append(send(gram.at[rows, right], gram.at[rows, right], dk=1))
    scopies[0].wait_recv()

    jobs = [
        [lambda: wide_first(4), lambda: narrow_step(1)],
        [lambda: wide_first(5)],
        [lambda: wide_first(6)],
        [lambda: narrow_first(), lambda: wide_first(7)],
        [],
        [lambda: narrow_second(), lambda: wide_first(0)],
        [],
        [lambda: narrow_gather(0), lambda: wide_second()],
        [],
        [lambda: narrow_gather(1)],
        [lambda: wide_third(1), lambda: wide_third(7)],
        [],
        [lambda: wide_third(2), lambda: wide_third(6)],
        [lambda: narrow_gather(2)],
        [lambda: wide_third(3), lambda: wide_third(5)],
        [lambda: wide_third(4), lambda: narrow_gather(3)],
    ]

    for b in range(NX):
        low, high = b * XS, (b + 1) * XS
        tiles = [gram[low + 8 * i : low + 8 * i + 8, low:high] for i in range(16)]
        for part in range(4):
            eliminate(tiles, range(4 * part, 4 * part + 4))
            for job in jobs[4 * b + part]:
                job()
        block = jnp.concatenate(tiles, axis=0)
        if b == 0:
            for copy in scopies[1:]:
                copy.wait_recv()
            for copy in list(zcopies.values()) + scopies:
                sent(copy)
        panel = exact(block, gram[low:high, :])
        gram[low:high, :] = panel
        gram[low:high, low:high] = block
        if b < NX - 1:
            factor = gram[low:high, high:].T
            cross = exact(factor, gram[low:high, :])
            old = gram[high:, :]
            spot_lane = lax.broadcasted_iota(I32, (RANK - high, RANK), 1)
            gram[high:, :] = jnp.where((spot_lane >= low) & (spot_lane < high), 0.0, old) - cross

    inverse = gram
    q_in = split(pf[...])
    for b in range(NX):
        high = (b + 1) * XS
        qb[:, b * XS : high] = dot3((q_in[0][:, :high], q_in[1][:, :high]), split(inverse[b * XS : high, :high]), NT)

    for copy in agx + [bgup[3], bgdown[3]]:
        copy.wait_recv()
    factors = [split(inverse[b * XS : (b + 1) * XS, : (b + 1) * XS]) for b in range(NX)]
    squares = [jnp.zeros((XS, 128), F32) for _ in range(NX)]
    for begin, count in PARTS:
        here = slice(begin, begin + count)
        high, low = split(wt[:, here])
        for b in range(NX):
            end = (b + 1) * XS
            rows = slice(b * XS, end)
            piece = dot3(factors[b], (high[:end], low[:end]))
            rt[rows, here] = piece
            for i in range(count // 128):
                squares[b] += piece[:, i * 128 : (i + 1) * 128] ** 2

    sub = lax.broadcasted_iota(I32, (8, 128), 0)
    packed = jnp.zeros((8, 128), F32)
    for b in range(NX):
        packed = jnp.where(sub == b, exact(jnp.ones((8, 128), F32), squares[b], NT), packed)
    sq[...] = packed
    copies = [send(sq, sqr.at[d - 1], dz=d) for d in zd]

    basis = qb[...].astype(BF16)
    for begin, count in PARTS:
        here = slice(begin, begin + count)
        high, low = split(rt[:, here])
        rh[:, here] = high
        rl[:, here] = low
        mom_new[:, here] = mom[:, here] - (1.0 - MOMENTUM_DECAY) * dot(basis, high)
    mom_copy = pltpu.make_async_copy(mom_new, mom_out, sems_l.at[1])
    mom_copy.start()
    for copy in copies:
        copy.wait_recv()
    for d in zd:
        packed = packed + sqr[d - 1]
    sqc[0] = packed
    send(sqc.at[0], sqc.at[1], dk=1).wait_recv()
    scales = lax.rsqrt((sqc[0] + sqc[1]) * (1.0 / COLS) + EPSILON)

    scale_row = jnp.concatenate([scales[b : b + 1, :] for b in range(NX)], axis=1)
    weight_copy.wait()
    scaled = split(qb[...] * (scale_row * (ROWS / RANK) ** 0.5))
    for begin, count in PARTS:
        here = slice(begin, begin + count)
        update = dot3(scaled, (rh[:, here], rl[:, here]))
        w_new[:, here] = (w_in[:, here].astype(F32) - rate[0] * update).astype(BF16)
    weight_out_copy = pltpu.make_async_copy(w_new, weight_out, sems_l.at[2])
    weight_out_copy.start()
    picked = lax.broadcasted_iota(I32, (SL, RANK), 1) == r * SL + lax.broadcasted_iota(I32, (SL, RANK), 0)
    own_scale = jnp.sum(jnp.where(picked, scale_row, 0.0), axis=1, keepdims=True)
    next_new[...] = rt[pl.ds(pl.multiple_of(r * SL, SL), SL), :] * own_scale
    next_copy = pltpu.make_async_copy(next_new, next_out, sems_l.at[3])
    next_copy.start()
    mom_copy.wait()
    weight_out_copy.wait()
    next_copy.wait()
    for copy in pending:
        copy.wait_send()


SENDS = 1 + 7 + 7 + 8 + 3 + 7 + 24 + 3 + 28 + 4 + 7 + 7 + 24 + 8 + 3 + 3 + 8 + 7 + 1


def per_device(momentum, weight, init_seed, step_rate):
    vmem, smem, anywhere = (pl.BlockSpec(memory_space=space) for space in (pltpu.VMEM, pltpu.SMEM, pl.ANY))
    return pl.pallas_call(
        update_tile,
        out_shape=[
            jax.ShapeDtypeStruct((TR, TC), F32),
            jax.ShapeDtypeStruct((TR, TC), BF16),
            jax.ShapeDtypeStruct((SL, TC), F32),
        ],
        in_specs=[vmem, anywhere, smem, smem],
        out_specs=[anywhere, anywhere, anywhere],
        scratch_shapes=[
            pltpu.VMEM((TR, TC), BF16),
            pltpu.VMEM((TR, TC), F32),
            pltpu.VMEM((TR, TC), BF16),
            pltpu.VMEM((SL, TC), F32),
            pltpu.VMEM((TR, RANK), F32),
            pltpu.VMEM((RANK, TC), F32),
            pltpu.VMEM((RANK, TC), BF16),
            pltpu.VMEM((RANK, TC), BF16),
            pltpu.VMEM((TR, TC), BF16),
            pltpu.VMEM((TR, TC), BF16),
            pltpu.VMEM((TC, RANK), BF16),
            pltpu.VMEM((TC, RANK), BF16),
            pltpu.VMEM((TR, RANK), F32),
            pltpu.VMEM((HALF, RANK), F32),
            pltpu.VMEM((HALF, RANK), F32),
            pltpu.VMEM((NZ - 1, PZ, RANK), F32),
            pltpu.VMEM((TR, RANK), F32),
            pltpu.VMEM((RANK, TR), F32),
            pltpu.VMEM((32, TR), F32),
            pltpu.VMEM((NX, 32, RANK), F32),
            pltpu.VMEM((8, RANK), F32),
            pltpu.VMEM((NY - 1, 8, RANK), F32),
            pltpu.VMEM((32, RANK), F32),
            pltpu.VMEM((RANK, RANK), F32),
            pltpu.VMEM((RANK, TC), F32),
            pltpu.VMEM((NX - 1, NY, SL, WIDE), F32),
            pltpu.VMEM((NY - 1, SL, WIDE), F32),
            pltpu.VMEM((NX - 1, SL, NARROW), F32),
            pltpu.VMEM((8, YS, NARROW), F32),
            pltpu.VMEM((RANK, TC), F32),
            pltpu.VMEM((8, 128), F32),
            pltpu.VMEM((NZ - 1, 8, 128), F32),
            pltpu.VMEM((2, 8, 128), F32),
            pltpu.SemaphoreType.DMA((SENDS,)),
            pltpu.SemaphoreType.DMA((SENDS,)),
            pltpu.SemaphoreType.DMA((4,)),
        ],
        compiler_params=pltpu.CompilerParams(collective_id=0, has_side_effects=True, vmem_limit_bytes=56 * 2**20),
        name="update_tile",
    )(momentum, weight, init_seed, step_rate)


def solution(mesh):
    placed = (P("row", "col"), P("row", "col"), P(), P())
    return jax.shard_map(
        per_device,
        mesh=mesh,
        in_specs=placed,
        out_specs=(P("row", "col"), P("row", "col"), P("row", "col")),
        check_vma=False,
    )
```

time: 186 us -> 133 us (0.72); the launches traced: 183 us -> 133 us
  Pallas kernels: 173 us -> 127 us
  local copies, waits for them, and re-layouts: 6.37 us -> 4.38 us
    pallas_call x2 -> x1, Pallas kernels: 173 us -> 127 us  [per_device(): pl.pallas_call(update_tile, out_shape=[jax.ShapeDtypeStruct((TR, TC), F32...]
    unnamed x12 -> x7, local copies, waits for them, and re-layouts: 6.29 us -> 4.38 us
where the time goes in v2:
time: 133 us
  Pallas kernels  127 us (95%)
  local copies, waits for them, and re-layouts  4.38 us (3%)
  between operations  1.95 us (1%)
    pallas_call x1, Pallas kernels, per_device(): pl.pallas_call(update_tile, out_shape=[jax.ShapeDtypeStruct((TR, TC), F32...  127 us
    unnamed x7, local copies, waits for them, and re-layouts  4.38 us

profile of v2, /device:TPU:1, one launch (start us, length us, event | category | flops | bytes accessed | tf_op | source)
XLA Modules:
  0.0 132.9 jit_solution(8589074265764904504)
XLA Ops:
  1.9 126.5 %update_tile.1 = (f32[256,1664]{1,0:T(8,128)}, bf16[256,1664]{1,0:T(8,128)(2,1)}, f32[16,1664]{1,0:T(8,128)}) custom-call(f32[256,1664]{1,0:T(8,128)} %mom.1, bf16[256,1664]{1,0:T(8,128)(2,1)} %weight_in.1, s32[1]{0:T(128)S(6)} %copy.10.seed, f32[1]{0:T(128)S(6)} %copy.11.rate), custom_call_target="tpu_custom_call" | custom-call | tf_op jit(solution)/shard_map/update_tile/pallas_call | solution.py:440
  128.5 0.0 copy-start
  128.5 0.0 copy-start.1
  128.5 2.8 %copy.12 = f32[256,1664]{1,0:T(8,128)} copy(f32[256,1664]{1,0:T(8,128)} %get-tuple-element.6) | data formatting | bytes 3407872
  131.3 0.0 copy-done
  131.3 0.9 copy.13
  132.2 0.0 copy-done.1
  132.2 0.6 copy.14
Async XLA Ops:
  128.5 2.9 %copy-start = (bf16[256,1664]{1,0:T(8,128)(2,1)S(1)}, bf16[256,1664]{1,0:T(8,128)(2,1)}, u32[]{:S(2)}) copy-start(bf16[256,1664]{1,0:T(8,128)(2,1)} %get-tuple-element.7) | copy-start | bytes 2555908
  128.5 3.7 %copy-start.1 = (f32[16,1664]{1,0:T(8,128)S(1)}, f32[16,1664]{1,0:T(8,128)}, u32[]{:S(2)}) copy-start(f32[16,1664]{1,0:T(8,128)} %get-tuple-element.8) | copy-start | bytes 319492

commit v3 on v2

--- a/solution.py
+++ b/solution.py
@@ -16,7 +16,8 @@
 TR, TC = 256, 1664
 WIDE = 1024
 NARROW = TC - WIDE
-LEFT = 384
+HW = WIDE // 2
+CHUNKS = ((0, 256, (4, 3)), (256, 256, (3, 4)), (512, 128, (4, 3)))
 XS = RANK // NX
 SL = XS // NY
 YS = RANK // NY
@@ -146,14 +147,15 @@
         mh[:, here] = high
         ml[:, here] = low
 
-    for half in range(2):
-        rows = slice(half * HALF, (half + 1) * HALF)
-        pp[rows, :] = dot3((mh[rows, :], ml[rows, :]), (vh[...], vl[...]))
+    mine = pl.ds(pl.multiple_of(k * HALF, HALF), HALF)
+    other = pl.ds(pl.multiple_of((1 - k) * HALF, HALF), HALF)
+    pp[...] = dot3((mh[other, :], ml[other, :]), (vh[...], vl[...]))
     pl.semaphore_wait(barrier, len(others))
 
-    mine = pl.ds(pl.multiple_of(k * HALF, HALF), HALF)
-    send(pp.at[pl.ds(pl.multiple_of((1 - k) * HALF, HALF), HALF)], ch, dk=1).wait_recv()
-    ph[...] = pp[mine, :] + ch[...]
+    half_copy = send(pp, ch, dk=1)
+    ph[...] = dot3((mh[mine, :], ml[mine, :]), (vh[...], vl[...]))
+    half_copy.wait_recv()
+    ph[...] += ch[...]
     copies = [send(ph.at[pl.ds(pl.multiple_of(lax.rem(z + d, NZ) * PZ, PZ), PZ)], zr.at[d - 1], dz=d) for d in zd]
     for copy in copies:
         copy.wait_recv()
@@ -185,8 +187,7 @@
         here = pl.ds(pl.multiple_of(i * XS, XS), XS)
         wp[here, :] = dot3(split(pt[here, :]), (mh[...], ml[...]))
 
-    wide, narrow = pl.ds(0, WIDE), pl.ds(WIDE, NARROW)
-    left, right_half = pl.ds(WIDE, LEFT), pl.ds(WIDE + LEFT, NARROW - LEFT)
+    order = (1, 7, 2, 6, 3, 5, 4, 0)
 
     def a_rows(dx, dy):
         return pl.ds(pl.multiple_of(lax.rem(x + dx, NX) * XS + lax.rem(y + dy, NY) * SL, SL), SL)
@@ -197,87 +198,100 @@
     def b_rows(dx):
         return pl.ds(pl.multiple_of(y * YS + lax.rem(x + dx, NX) * SL, SL), SL)
 
-    xcopies, ycopies, agy, agx, bup, bdown, bxc, bgx, bgup, bgdown = {}, {}, {}, [], {}, {}, [], [], {}, {}
-
-    def wide_start(es):
+    xcopies, ycopies, agy, agx, ring, bxc, bgx, bgather = {}, {}, {}, [], {}, {}, {}, {}
+
+    halves = (pl.ds(0, HW), pl.ds(HW, HW))
+
+    def wide_start(h):
+        for e in order:
+            for d in xd:
+                xcopies[h, e, d] = send(wp.at[a_rows(d, e), halves[h]], xr.at[h, d - 1, e], dx=d)
+
+    def wide_first(h, *es):
         for e in es:
             for d in xd:
-                xcopies[e, d] = send(wp.at[a_rows(d, e), wide], xr.at[d - 1, e], dx=d)
-
-    def wide_first(e):
+                xcopies[h, e, d].wait_recv()
+            rows = a_rows(0, e)
+            total = wp[rows, halves[h]]
+            for d in xd:
+                total = total + xr[h, d - 1, e]
+            wp[rows, halves[h]] = total
+            if e:
+                ycopies[h, e] = send(wp.at[rows, halves[h]], yr.at[h, e - 1], dy=e)
+
+    def wide_second(h):
+        for e in yd:
+            ycopies[h, e].wait_recv()
+        rows = a_rows(0, 0)
+        total = wp[rows, halves[h]]
+        for e in yd:
+            total = total + yr[h, e - 1]
+        wt[rows, halves[h]] = total
         for d in xd:
-            xcopies[e, d].wait_recv()
-        rows = a_rows(0, e)
-        total = wp[rows, wide]
-        for d in xd:
-            total = total + xr[d - 1, e]
-        wp[rows, wide] = total
-        if e:
-            ycopies[e] = send(wp.at[rows, wide], yr.at[e - 1], dy=e)
-
-    def wide_second():
-        for e in yd:
-            ycopies[e].wait_recv()
-        rows = a_rows(0, 0)
-        total = wp[rows, wide]
-        for e in yd:
-            total = total + yr[e - 1]
-        wt[rows, wide] = total
-        for d in xd:
-            agx.append(send(wt.at[rows, wide], wt.at[rows, wide], dx=d))
+            agx.append(send(wt.at[rows, halves[h]], wt.at[rows, halves[h]], dx=d))
         for e in (1, 7, 2, 6, 3, 5, 4):
-            agy[e] = send(wt.at[rows, wide], wt.at[rows, wide], dy=e)
-
-    def wide_third(e):
-        agy[e].wait_recv()
-        rows = a_rows(0, NY - e)
-        for d in xd:
-            agx.append(send(wt.at[rows, wide], wt.at[rows, wide], dx=d))
+            agy[h, e] = send(wt.at[rows, halves[h]], wt.at[rows, halves[h]], dy=e)
+
+    def wide_third(h, *es):
+        for e in es:
+            agy[h, e].wait_recv()
+            rows = a_rows(0, NY - e)
+            for d in xd:
+                agx.append(send(wt.at[rows, halves[h]], wt.at[rows, halves[h]], dx=d))
+
+    chunks = [(i, pl.ds(WIDE + begin, count), pl.ds(begin, count), reach) for i, (begin, count, reach) in enumerate(CHUNKS)]
+    ways = ((1, 1), (NY - 1, -1))
+
+    def block_at(way, d):
+        return b_block(d if way[1] > 0 else NY - d)
+
+    def narrow_send(i, cols, slot, w, d):
+        ring[i, w, d] = send(wp.at[block_at(ways[w], d), cols], by.at[w, d - 1, :, slot], dy=ways[w][0])
 
     def narrow_start():
-        bup[4] = send(wp.at[b_block(4), left], by.at[0, :, pl.ds(0, LEFT)], dy=1)
-        bdown[4] = send(wp.at[b_block(4), right_half], by.at[4, :, pl.ds(LEFT, NARROW - LEFT)], dy=NY - 1)
-
-    def narrow_step(d):
-        bup[d + 1].wait_recv()
-        bdown[d + 1].wait_recv()
-        if d == 3:
-            wp[b_block(3), left] += by[0, :, 0:LEFT]
-            wp[b_block(5), right_half] += by[4, :, LEFT:NARROW]
-        else:
-            wp[b_block(d), narrow] += by[3 - d]
-            wp[b_block(NY - d), narrow] += by[7 - d]
-        bup[d] = send(wp.at[b_block(d), narrow], by.at[4 - d], dy=1)
-        bdown[d] = send(wp.at[b_block(NY - d), narrow], by.at[8 - d], dy=NY - 1)
+        for i, cols, slot, reach in chunks:
+            for w in range(2):
+                narrow_send(i, cols, slot, w, reach[w])
+
+    def narrow_step(level):
+        for i, cols, slot, reach in chunks:
+            for w in range(2):
+                d = reach[w] - level
+                if d >= 1:
+                    ring[i, w, d + 1].wait_recv()
+                    wp[block_at(ways[w], d), cols] += by[w, d, :, slot]
+                    narrow_send(i, cols, slot, w, d)
 
     def narrow_first():
-        bup[1].wait_recv()
-        bdown[1].wait_recv()
-        wp[b_block(0), narrow] += by[3] + by[7]
-        for d in xd:
-            bxc.append(send(wp.at[b_rows(d), narrow], bx.at[d - 1], dx=d))
+        for i, cols, slot, reach in chunks:
+            for w in range(2):
+                ring[i, w, 1].wait_recv()
+            wp[b_block(0), cols] += by[0, 0, :, slot] + by[1, 0, :, slot]
+            for d in xd:
+                bxc[i, d] = send(wp.at[b_rows(d), cols], bx.at[d - 1, :, slot], dx=d)
 
     def narrow_second():
-        for copy in bxc:
-            copy.wait_recv()
-        rows = b_rows(0)
-        total = wp[rows, narrow]
-        for d in xd:
-            total = total + bx[d - 1]
-        wt[rows, narrow] = total
-        for d in xd:
-            bgx.append(send(wt.at[rows, narrow], wt.at[rows, narrow], dx=d))
-
-    def narrow_gather(d):
-        if d == 0:
-            for copy in bgx:
-                copy.wait_recv()
-        else:
-            bgup[d - 1].wait_recv()
-            bgdown[d - 1].wait_recv()
-        up, down = (left, right_half) if d == 3 else (narrow, narrow)
-        bgup[d] = send(wt.at[b_block(NY - d if d else 0), up], wt.at[b_block(NY - d if d else 0), up], dy=1)
-        bgdown[d] = send(wt.at[b_block(d), down], wt.at[b_block(d), down], dy=NY - 1)
+        for i, cols, slot, reach in chunks:
+            rows = b_rows(0)
+            total = wp[rows, cols]
+            for d in xd:
+                bxc[i, d].wait_recv()
+                total = total + bx[d - 1, :, slot]
+            wt[rows, cols] = total
+            for d in xd:
+                bgx[i, d] = send(wt.at[rows, cols], wt.at[rows, cols], dx=d)
+
+    def narrow_gather(level):
+        for i, cols, slot, reach in chunks:
+            if level == 0:
+                for d in xd:
+                    bgx[i, d].wait_recv()
+            for w in range(2):
+                if level < reach[w]:
+                    if level:
+                        bgather[i, w, level - 1].wait_recv()
+                    rows = b_block(level if w else NY - level) if level else b_block(0)
+                    bgather[i, w, level] = send(wt.at[rows, cols], wt.at[rows, cols], dy=ways[w][0])
 
     for copy in gcopies:
         copy.wait_recv()
@@ -286,8 +300,11 @@
         total = total + gx[d, 0:8, :]
     g1[...] = total
     gcopies = [send(g1, gy.at[d - 1], dy=d) for d in yd]
-    wide_start((1, 2, 3))
+    wide_start(0)
     narrow_start()
+    wide_first(0, 1, 7)
+    narrow_step(1)
+    wide_first(0, 2)
     for copy in gcopies:
         copy.wait_recv()
     total = g1[...]
@@ -296,9 +313,8 @@
     own = pl.ds(pl.multiple_of(x * 8, 8), 8)
     gs[own, :] = total
     gcopies = [send(gs.at[own], gs.at[own], dx=d) for d in xd]
-    wide_start((4, 5, 6, 7, 0))
-    narrow_step(3)
-    wide_first(1)
+    wide_start(1)
+    wide_first(0, 6, 3, 5, 4)
     for copy in gcopies:
         copy.wait_recv()
 
@@ -312,9 +328,13 @@
         right = pl.ds(i * XS, RANK - i * XS)
         for d in zd:
             zcopies[i, d] = send(gram.at[g_rows(i, k, 0), right], gram.at[g_rows(i, k, 0), right], dz=d)
-    wide_first(2)
     narrow_step(2)
-    wide_first(3)
+    wide_first(0, 0)
+    wide_first(1, 1, 7)
+    wide_second(0)
+    narrow_step(3)
+    wide_first(1, 2, 6)
+    wide_third(0, 1, 7)
     scopies = []
     for i in range(NX):
         right = pl.ds(i * XS, RANK - i * XS)
@@ -325,22 +345,22 @@
     scopies[0].wait_recv()
 
     jobs = [
-        [lambda: wide_first(4), lambda: narrow_step(1)],
-        [lambda: wide_first(5)],
-        [lambda: wide_first(6)],
-        [lambda: narrow_first(), lambda: wide_first(7)],
+        [lambda: narrow_first(), lambda: wide_first(1, 3, 5), lambda: wide_third(0, 2, 6)],
+        [lambda: wide_first(1, 4)],
+        [lambda: narrow_second(), lambda: wide_third(0, 3, 5), lambda: wide_first(1, 0)],
+        [lambda: wide_third(0, 4)],
+        [lambda: narrow_gather(0), lambda: wide_second(1)],
         [],
-        [lambda: narrow_second(), lambda: wide_first(0)],
+        [lambda: wide_third(1, 1, 7)],
+        [lambda: narrow_gather(1), lambda: wide_third(1, 2, 6)],
         [],
-        [lambda: narrow_gather(0), lambda: wide_second()],
+        [lambda: wide_third(1, 3, 5)],
+        [lambda: narrow_gather(2), lambda: wide_third(1, 4)],
         [],
-        [lambda: narrow_gather(1)],
-        [lambda: wide_third(1), lambda: wide_third(7)],
         [],
-        [lambda: wide_third(2), lambda: wide_third(6)],
-        [lambda: narrow_gather(2)],
-        [lambda: wide_third(3), lambda: wide_third(5)],
-        [lambda: wide_third(4), lambda: narrow_gather(3)],
+        [lambda: narrow_gather(3)],
+        [],
+        [],
     ]
 
     for b in range(NX):
@@ -372,7 +392,7 @@
         high = (b + 1) * XS
         qb[:, b * XS : high] = dot3((q_in[0][:, :high], q_in[1][:, :high]), split(inverse[b * XS : high, :high]), NT)
 
-    for copy in agx + [bgup[3], bgdown[3]]:
+    for copy in agx + [bgather[i, w, reach[w] - 1] for i, _, _, reach in chunks for w in range(2)]:
         copy.wait_recv()
     factors = [split(inverse[b * XS : (b + 1) * XS, : (b + 1) * XS]) for b in range(NX)]
     squares = [jnp.zeros((XS, 128), F32) for _ in range(NX)]
@@ -432,7 +452,7 @@
         copy.wait_send()
 
 
-SENDS = 1 + 7 + 7 + 8 + 3 + 7 + 24 + 3 + 28 + 4 + 7 + 7 + 24 + 8 + 3 + 3 + 8 + 7 + 1
+SENDS = 1 + 7 + 7 + 8 + 3 + 7 + 48 + 3 + 28 + 4 + 14 + 14 + 48 + 3 * (7 + 3 + 3 + 7) + 7 + 1
 
 
 def per_device(momentum, weight, init_seed, step_rate):
@@ -459,7 +479,7 @@
             pltpu.VMEM((TR, TC), BF16),
             pltpu.VMEM((TC, RANK), BF16),
             pltpu.VMEM((TC, RANK), BF16),
-            pltpu.VMEM((TR, RANK), F32),
+            pltpu.VMEM((HALF, RANK), F32),
             pltpu.VMEM((HALF, RANK), F32),
             pltpu.VMEM((HALF, RANK), F32),
             pltpu.VMEM((NZ - 1, PZ, RANK), F32),
@@ -472,10 +492,10 @@
             pltpu.VMEM((32, RANK), F32),
             pltpu.VMEM((RANK, RANK), F32),
             pltpu.VMEM((RANK, TC), F32),
-            pltpu.VMEM((NX - 1, NY, SL, WIDE), F32),
-            pltpu.VMEM((NY - 1, SL, WIDE), F32),
+            pltpu.VMEM((2, NX - 1, NY, SL, HW), F32),
+            pltpu.VMEM((2, NY - 1, SL, HW), F32),
             pltpu.VMEM((NX - 1, SL, NARROW), F32),
-            pltpu.VMEM((8, YS, NARROW), F32),
+            pltpu.VMEM((2, 4, YS, NARROW), F32),
             pltpu.VMEM((RANK, TC), F32),
             pltpu.VMEM((8, 128), F32),
             pltpu.VMEM((NZ - 1, 8, 128), F32),

time: 133 us -> 125 us (0.940)
  Pallas kernels: 127 us -> 119 us
    pallas_call x1, Pallas kernels: 127 us -> 119 us  [per_device(): pl.pallas_call(update_tile, out_shape=[jax.ShapeDtypeStruct((TR, TC), F32...]
where the time goes in v3:
time: 125 us
  Pallas kernels  119 us (95%)
  local copies, waits for them, and re-layouts  4.38 us (4%)
  between operations  1.95 us (2%)
    pallas_call x1, Pallas kernels, per_device(): pl.pallas_call(update_tile, out_shape=[jax.ShapeDtypeStruct((TR, TC), F32...  119 us
    unnamed x7, local copies, waits for them, and re-layouts  4.38 us

profile of v3, /device:TPU:1, one launch (start us, length us, event | category | flops | bytes accessed | tf_op | source)
XLA Modules:
  0.0 125.0 jit_solution(17158278361463944209)
XLA Ops:
  1.9 118.7 %update_tile.1 = (f32[256,1664]{1,0:T(8,128)}, bf16[256,1664]{1,0:T(8,128)(2,1)}, f32[16,1664]{1,0:T(8,128)}) custom-call(f32[256,1664]{1,0:T(8,128)} %mom.1, bf16[256,1664]{1,0:T(8,128)(2,1)} %weight_in.1, s32[1]{0:T(128)S(6)} %copy.10.seed, f32[1]{0:T(128)S(6)} %copy.11.rate), custom_call_target="tpu_custom_call" | custom-call | tf_op jit(solution)/shard_map/update_tile/pallas_call | solution.py:460
  120.6 0.0 copy-start
  120.7 0.0 copy-start.1
  120.7 2.8 %copy.12 = f32[256,1664]{1,0:T(8,128)} copy(f32[256,1664]{1,0:T(8,128)} %get-tuple-element.6) | data formatting | bytes 3407872
  123.5 0.0 copy-done
  123.5 0.9 copy.13
  124.4 0.0 copy-done.1
  124.4 0.6 copy.14
Async XLA Ops:
  120.6 2.9 %copy-start = (bf16[256,1664]{1,0:T(8,128)(2,1)S(1)}, bf16[256,1664]{1,0:T(8,128)(2,1)}, u32[]{:S(2)}) copy-start(bf16[256,1664]{1,0:T(8,128)(2,1)} %get-tuple-element.7) | copy-start | bytes 2555908
  120.7 3.7 %copy-start.1 = (f32[16,1664]{1,0:T(8,128)S(1)}, f32[16,1664]{1,0:T(8,128)}, u32[]{:S(2)}) copy-start(f32[16,1664]{1,0:T(8,128)} %get-tuple-element.8) | copy-start | bytes 319492
